TPU v7x, 256 devices: a whole 4x4x8 slice. The times are simulated.
256 devices in a mesh: front: 16 (over z, core), tile: 16 (over y, x).
Axes of the slice: x: 4, y: 4, z: 8, core: 2. Of those that a mesh axis runs over, the one named last changes fastest.
Arguments:
- parent_solution: bfloat16 [16, 64, 256, 512], P('tile', 'front'), may hold values from -6 to 6
- segment_ids: int32 [16, 16, 16], P('tile'), may hold values from 0 to 63, as said below
- segment_counts: int32 [16, 16, 2], P('tile'), may hold values from 4 to 8
- row_bases: bfloat16 [16, 16, 2, 8, 16, 64, 256], P('tile', 'front'), may hold values from -0.03125 to 0.03125
- column_bases: bfloat16 [16, 2, 16, 64, 256], P('front', None, 'tile'), may hold values from -0.75 to 0.75
- diag_inverse: bfloat16 [16, 2, 16, 256, 256], P('front', None, 'tile'), may hold values from -0.375 to 0.375
- child_right: bfloat16 [16, 2, 16, 256, 512], P('front', None, 'tile'), may hold values from -6 to 6
- tile_ranks: int32 [16, 2, 16], P('front', None, 'tile'), may hold values from 8 to 64
Outputs:
- child_solution: bfloat16 [16, 2, 16, 256, 512], P('front', None, 'tile')
Inputs may be any that keep to these rules, and one draw needn't show every extreme that they name: `segment_ids`: block id // 4 is the front index holding the block. In every row of 16 ids no front index holds more than 2 of the named blocks, and one holds exactly 2.
All inputs are finite; a program needn't handle non-finite values.
Results may differ from a plain program's by a relative error of at most 0.0052.
Values may be sent and summed in bfloat16 or wider, within the bound.
A program may use at most 128 MiB of HBM per device.

v0:
```python
import jax
import jax.numpy as jnp
from jax import lax
from jax.sharding import PartitionSpec as P

CAP = 2


def local(
    parent_solution,
    segment_ids,
    segment_counts,
    row_bases,
    column_bases,
    diag_inverse,
    child_right,
    tile_ranks,
):
    nfront = lax.axis_size("front")
    my_front = lax.axis_index("front")
    held_blocks = parent_solution[0]
    per_owner = held_blocks.shape[0]
    block_ids = segment_ids[0]
    counts_here = segment_counts[0]
    need_slots = block_ids.shape[1]
    fronts_here = counts_here.shape[1]
    seg_slots = need_slots // fronts_here
    slot_index = jnp.arange(need_slots)
    usable = (slot_index % seg_slots)[None, :] < jnp.repeat(counts_here, seg_slots, axis=1)
    owner_front = block_ids // per_owner
    local_block = block_ids % per_owner
    same_owner = owner_front[:, :, None] == owner_front[:, None, :]
    before = slot_index[None, :, None] > slot_index[None, None, :]
    position = jnp.sum((same_owner & before & usable[:, None, :]).astype(jnp.int32), axis=2)
    mine_here = usable & (owner_front == my_front)
    pick_slot = (
        (position[:, :, None] == jnp.arange(CAP)[None, None, :]) & mine_here[:, :, None]
    ).astype(jnp.float32)
    pick_local = (local_block[:, :, None] == jnp.arange(per_owner)[None, None, :]).astype(
        jnp.float32
    )
    selector = jnp.einsum("fsp,fsl->fpl", pick_slot, pick_local).astype(jnp.bfloat16)
    outgoing = jnp.einsum(
        "fpl,lbr->fpbr", selector, held_blocks, preferred_element_type=jnp.float32
    ).astype(jnp.bfloat16)
    owner_me = lax.dynamic_index_in_dim(owner_front, my_front, 0, keepdims=False)
    position_me = lax.dynamic_index_in_dim(position, my_front, 0, keepdims=False)
    usable_me = lax.dynamic_index_in_dim(usable, my_front, 0, keepdims=False)
    source_slot = owner_me * CAP + position_me
    receiver_pick = (
        (source_slot[:, None] == jnp.arange(nfront * CAP)[None, :]) & usable_me[:, None]
    ).astype(jnp.bfloat16)
    bases_here = row_bases[0, 0]
    nblock = held_blocks.shape[1]
    ncols = held_blocks.shape[2]
    received = lax.all_to_all(outgoing, "front", split_axis=0, concat_axis=0, tiled=True)
    arrived = received.reshape(nfront * CAP, nblock, ncols // 128, 128)
    gathered = jnp.einsum(
        "sq,qbmn->sbmn", receiver_pick, arrived, preferred_element_type=jnp.float32
    ).astype(jnp.bfloat16)
    gathered = gathered.reshape(fronts_here, seg_slots, nblock, arrived.shape[2], arrived.shape[3])
    partial_value = jnp.einsum(
        "csjkb,csbmn->cjkmn", bases_here, gathered, preferred_element_type=jnp.float32
    )
    partial_value = partial_value.reshape(
        fronts_here, partial_value.shape[1], partial_value.shape[2], ncols
    )
    own_part = lax.psum_scatter(partial_value, "tile", scatter_dimension=1, tiled=True)
    rank_here = tile_ranks[0]
    keep = jnp.arange(own_part.shape[2])[None, None, :, None] < rank_here[:, :, None, None]
    rank_space = (own_part * keep.astype(jnp.float32)).astype(jnp.bfloat16)
    projected = jnp.einsum(
        "cjkb,cjkr->cjbr", column_bases[0], rank_space, preferred_element_type=jnp.float32
    )
    reduced = (child_right[0].astype(jnp.float32) - projected).astype(jnp.bfloat16)
    solved = jnp.einsum(
        "cjab,cjbr->cjar", diag_inverse[0], reduced, preferred_element_type=jnp.float32
    )
    return solved.astype(jnp.bfloat16)[None]


def solution(mesh):
    placed = (
        P("tile", "front", None, None),
        P("tile", None, None),
        P("tile", None, None),
        P("tile", "front", None, None, None, None, None),
        P("front", None, "tile", None, None),
        P("front", None, "tile", None, None),
        P("front", None, "tile", None, None),
        P("front", None, "tile"),
    )
    return jax.shard_map(
        local,
        mesh=mesh,
        in_specs=placed,
        out_specs=P("front", None, "tile", None, None),
        check_vma=False,
    )
```

profile of v0, /device:TPU:1, one launch (start us, length us, event | category | flops | bytes accessed | tf_op | source)
XLA Modules:
  0.0 393.1 jit_solution(3212064493065103912)
XLA Ops:
  6.5 0.7 broadcast_bitcast_fusion
  7.3 0.1 copy.64
  7.3 0.7 add_select_fusion
  8.0 0.7 compare_and_fusion.2
  8.8 0.4 convert_reduce_fusion
  9.2 0.1 fusion.8
  9.3 6.8 %convolution_convert_fusion = bf16[16,2,256,512]{3,0,2,1:T(8,128)(2,1)} fusion(bf16[4,256,512]{2,1,0:T(8,128)(2,1)} %bitcast.104, bf16[16,2,4,1]{2,1,0,3:T(2,128)(2,1)S(1)} %fusion.8), kind=kOutput, calls=%fused_computation | convolution fusion | flops 37748736 | bytes 9437440 | tf_op jit(solution)/shard_map/fpl,lbr->fpbr/dot_general | solution.py:43
  16.1 11.3 %copy.67 = bf16[16,2,256,512]{3,2,1,0:T(8,128)(2,1)} copy(bf16[16,2,256,512]{3,0,2,1:T(8,128)(2,1)} %convolution_convert_fusion) | data formatting | bytes 16777216 | tf_op jit(solution)/shard_map/convert_element_type | solution.py:45
  27.4 10.0 %all-to-all-start = ((bf16[16,2,256,512]{3,2,1,0:T(8,128)(2,1)}), bf16[16,2,256,512]{3,2,1,0:T(8,128)(2,1)}, u32[]{:S(2)}, u32[]{:S(2)}) async-start(bf16[16,2,256,512]{3,2,1,0:T(8,128)(2,1)} %copy.67), calls=%async_computation | async-start | bytes 16777216 | tf_op jit(solution)/shard_map/all_to_all | solution.py:56
  37.4 0.2 all-reduce.3.cloned.1.call-start
  37.7 16.9 %copy.77 = bf16[2,8,16,64,256,1]{3,1,4,2,5,0:T(8,128)(2,1)} copy(bf16[2,8,16,64,256,1]{4,3,2,1,0,5:T(8,128)(2,1)} %bitcast.103) | data formatting | bytes 16777216 | tf_op jit(solution)/shard_map/squeeze | solution.py:53
  54.6 166.4 %all-to-all-done = bf16[16,2,256,512]{3,2,1,0:T(8,128)(2,1)} async-done(((bf16[16,2,256,512]{3,2,1,0:T(8,128)(2,1)}), bf16[16,2,256,512]{3,2,1,0:T(8,128)(2,1)}, u32[]{:S(2)}, u32[]{:S(2)}) %all-to-all-start) | async-done | bytes 8388640 | tf_op jit(solution)/shard_map/all_to_all | solution.py:56
  221.0 12.3 %copy.68 = bf16[16,2,256,512]{2,3,1,0:T(8,128)(2,1)} copy(bf16[16,2,256,512]{3,2,1,0:T(8,128)(2,1)} %all-to-all-done) | data formatting | bytes 16777216 | tf_op jit(solution)/shard_map/all_to_all | solution.py:56
  233.2 14.6 %copy.69 = bf16[32,256,4,128]{3,0,2,1:T(8,128)(2,1)} copy(bf16[32,256,4,128]{1,3,2,0:T(8,128)(2,1)} %bitcast.101) | data formatting | bytes 16777216 | tf_op jit(solution)/shard_map/reshape | solution.py:57
  247.9 6.6 %convert_bitcast_fusion = bf16[2,8,256,4,128,1]{4,1,0,3,2,5:T(8,128)(2,1)} fusion(bf16[32,256,4,128]{3,0,2,1:T(8,128)(2,1)} %copy.69, s32[16]{0:T(128)S(1)} %fusion.39, pred[16]{0:T(512)(128)(4,1)S(1)} %dynamic-slice_bitcast_fusion), kind=kOutput, calls=%fused_computation.4 | convolution fusion | flops 136315904 | bytes 12582992 | tf_op jit(solution)/shard_map/sq,qbmn->sbmn/dot_general | solution.py:58
  254.5 10.9 %fusion.2 = f32[2,4,16,8,8,128]{5,4,3,2,1,0:T(8,128)} fusion(bf16[2,8,16,64,256,1]{3,1,4,2,5,0:T(8,128)(2,1)} %copy.77, bf16[2,8,256,4,128,1]{4,1,0,3,2,5:T(8,128)(2,1)} %convert_bitcast_fusion), kind=kOutput, calls=%fused_computation.5 | convolution fusion | flops 4294967296 | bytes 16777216 | tf_op jit(solution)/shard_map/csjkb,csbmn->cjkmn/dot_general | solution.py:62
  265.4 4.7 %copy.99 = f32[2,4,16,8,8,128]{5,4,1,3,2,0:T(8,128)} copy(f32[2,4,16,8,8,128]{5,4,3,2,1,0:T(8,128)} %fusion.2) | data formatting | bytes 8388608 | tf_op jit(solution)/shard_map/reshape | solution.py:65
  270.2 0.0 all-reduce.3.cloned.1.call-update
  270.2 0.2 copy.63
  270.4 0.6 dynamic-slice
  271.0 0.1 compare_convert_fusion
  271.1 112.0 %all-reduce.3.cloned.1.call-done = f32[2,16,64,512]{3,2,1,0:T(8,128)} async-done(((f32[2,16,64,512]{3,2,1,0:T(8,128)}), f32[2,16,64,512]{3,2,1,0:T(8,128)}) %all-reduce.3.cloned.1.call-update) | async-done | bytes 4194320
  383.1 2.1 fusion.7
  385.3 1.0 copy.73
  (13 shorter events, 0.0 us)
Async XLA Ops:
  6.5 376.6 %copy-start = (bf16[1,2,1,256,256]{4,3,2,1,0:T(8,128)(2,1)S(1)}, bf16[1,2,1,256,256]{4,3,2,1,0:T(8,128)(2,1)}, u32[]{:S(2)}) copy-start(bf16[1,2,1,256,256]{4,3,2,1,0:T(8,128)(2,1)} %param.13) | copy-start | bytes 786436
  27.4 193.5 %all-to-all-start = ((bf16[16,2,256,512]{3,2,1,0:T(8,128)(2,1)}), bf16[16,2,256,512]{3,2,1,0:T(8,128)(2,1)}, u32[]{:S(2)}, u32[]{:S(2)}) async-start(bf16[16,2,256,512]{3,2,1,0:T(8,128)(2,1)} %copy.67), calls=%async_computation | async-start | bytes 16777216 | tf_op jit(solution)/shard_map/all_to_all | solution.py:56
  37.4 345.7 %all-reduce.3.cloned.1.call-start = ((), (), s32[]{:S(2)}) async-start(), calls=%async_computation.1 | async-start | bytes 8388608
  265.4 4.8 %copy-start.1 = (bf16[1,2,1,256,512]{4,3,2,1,0:T(8,128)(2,1)S(1)}, bf16[1,2,1,256,512]{4,3,2,1,0:T(8,128)(2,1)}, u32[]{:S(2)}) copy-start(bf16[1,2,1,256,512]{4,3,2,1,0:T(8,128)(2,1)} %param.14) | copy-start | bytes 1572868
  265.4 5.0 %copy-start.4 = (u32[256]{0:T(256)S(1)}, u32[256]{0:T(256)}, u32[]{:S(2)}) copy-start(u32[256]{0:T(256)} %constant.71) | copy-start | bytes 3076
  265.4 5.6 %copy-start.3 = (s32[1,2,1]{1,2,0:T(1,128)S(1)}, s32[1,2,1]{1,2,0:T(1,128)}, u32[]{:S(2)}) copy-start(s32[1,2,1]{1,2,0:T(1,128)} %param.15) | copy-start | bytes 28
  265.4 117.7 %copy-start.2 = (bf16[1,2,1,64,256]{4,3,2,1,0:T(8,128)(2,1)S(1)}, bf16[1,2,1,64,256]{4,3,2,1,0:T(8,128)(2,1)}, u32[]{:S(2)}) copy-start(bf16[1,2,1,64,256]{4,3,2,1,0:T(8,128)(2,1)} %param.12) | copy-start | bytes 196612
Sparse Core Ops, SparseCore 0:
  270.3 112.7 all-reduce.2
where the time goes:
time: 394 us; the launch traced here: 393 us
  waiting for transfers between devices  278 us (71%)
  local copies, waits for them, and re-layouts  62.5 us (16%)
  matrix products  26.6 us (7%)
  between operations  13.5 us (3%)
  starting transfers between devices  10.2 us (3%)
    all_to_all x1, waiting for transfers between devices, local(): lax.all_to_all(outgoing, 'front', split_axis=0, concat_axis=0, tiled=True)  166 us
    unnamed x2, waiting for transfers between devices  112 us
    squeeze x1, local copies, waits for them, and re-layouts, local(): bases_here = row_bases[0, 0]  16.9 us
    reshape x1, local copies, waits for them, and re-layouts, local(): arrived = received.reshape(nfront * CAP, nblock, ncols // 128, 128)  14.6 us
    all_to_all x1, local copies, waits for them, and re-layouts, local(): lax.all_to_all(outgoing, 'front', split_axis=0, concat_axis=0, tiled=True)  12.3 us
    convert_element_type x1, local copies, waits for them, and re-layouts, local(): outgoing = jnp.einsum('fpl,lbr->fpbr', selector, held_blocks, preferred_e...  11.3 us
    dot_general x1, matrix products, local(): jnp.einsum('csjkb,csbmn->cjkmn', bases_here, gathered, preferred_element_...  10.9 us
    all_to_all x1, starting transfers between devices, local(): lax.all_to_all(outgoing, 'front', split_axis=0, concat_axis=0, tiled=True)  9.98 us
  transfers between devices with their start and end apart: 2, of which 2 were waited for; matrix products, arithmetic and copies ran while one was open for 5% of the time, Pallas kernels for 0%

commit v1 on v0

v1 whole, which is shorter than its diff:
```python
import functools

import jax
import jax.numpy as jnp
from jax import lax
from jax.experimental import pallas as pl
from jax.experimental.pallas import tpu as pltpu
from jax.sharding import PartitionSpec as P

MESH = pl.DeviceIdType.MESH

NZ = 8
NY = 4
NX = 4
NT = NY * NX
OWNED = 4
BLOCK = 256
RANK = 64
RHS = 512
SEG = 8
FRONTS = 2
WIDTH = 128
CHUNKS = RHS // WIDTH
NBLK = NZ * 2 * OWNED
GROUP = NX * RANK
PIECES = ((1, 0), (1, 1), (2, 0), (2, 1), (3, 0), (3, 1), (4, 0))
NP = len(PIECES)


def kernel(
    ids, counts, ranks, parent, bases, cols, diag, right_side, out,
    b0, b1, b2, b3, bases_v, cols_v, diag_v, right_v, out_v, part, arrived,
    ring_send, ring_recv, pair_send, pair_recv, tile_send, tile_recv, load_sem, own_sem, out_sem,
):
    blocks = (b0, b1, b2, b3)
    front = lax.axis_index("front")
    tile = lax.axis_index("tile")
    z, core = front // 2, front % 2
    y, x = tile // NX, tile % NX
    sibling = z * 2 + (1 - core)
    ahead = ((z + 1) % NZ) * 2 + core
    behind = ((z + NZ - 1) % NZ) * 2 + core

    def peer(k):
        return ((y + k // NX) % NY) * NX + (x + k % NX) % NX

    barrier = pltpu.get_barrier_semaphore()
    for other in (ahead, behind, sibling):
        pl.semaphore_signal(barrier, inc=1, device_id={"front": other}, device_id_type=MESH)
    for k in range(1, NT):
        pl.semaphore_signal(barrier, inc=1, device_id={"tile": peer(k)}, device_id_type=MESH)
    pl.semaphore_wait(barrier, 3 + NT - 1)

    def place(chip, who, half):
        return pl.ds((chip * 2 + who) * OWNED + half * 2, 2)

    def chunk_cols(r):
        return pl.ds(r * WIDTH, WIDTH)

    def ring(r, i, way):
        hop, half = PIECES[i]
        half = half if way == 0 else 1 - half
        chip = (z + NZ - (hop - 1)) % NZ if way == 0 else (z + hop - 1) % NZ
        dst = blocks[r].at[place(chip, core, half)]
        if hop == 1:
            src = parent.at[pl.ds(half * 2, 2), :, chunk_cols(r)]
        else:
            src = dst
        return pltpu.make_async_remote_copy(
            src_ref=src, dst_ref=dst,
            send_sem=ring_send.at[r, i, way], recv_sem=ring_recv.at[r, i, way],
            device_id={"front": ahead if way == 0 else behind}, device_id_type=MESH,
        )

    def ring_in(r, i, way, who):
        hop, half = PIECES[i]
        half = half if way == 0 else 1 - half
        chip = (z + NZ - hop) % NZ if way == 0 else (z + hop) % NZ
        return blocks[r].at[place(chip, who, half)]

    def wait_ring(r, i, way):
        here = ring_in(r, i, way, core)
        pltpu.make_async_remote_copy(
            src_ref=here, dst_ref=here,
            send_sem=ring_send.at[r, i, way], recv_sem=ring_recv.at[r, i, way],
            device_id={"front": ahead}, device_id_type=MESH,
        ).wait_recv()

    def pair(r, i, way, who):
        here = ring_in(r, i, way, who)
        return pltpu.make_async_remote_copy(
            src_ref=here, dst_ref=here,
            send_sem=pair_send.at[r, i, way], recv_sem=pair_recv.at[r, i, way],
            device_id={"front": sibling}, device_id_type=MESH,
        )

    def pair_own(r, who):
        return pltpu.make_async_remote_copy(
            src_ref=parent.at[:, :, chunk_cols(r)],
            dst_ref=blocks[r].at[pl.ds((z * 2 + who) * OWNED, OWNED)],
            send_sem=pair_send.at[r, NP, 0], recv_sem=pair_recv.at[r, NP, 0],
            device_id={"front": sibling}, device_id_type=MESH,
        )

    def keep_own(r):
        return pltpu.make_async_copy(
            parent.at[:, :, chunk_cols(r)], blocks[r].at[pl.ds(front * OWNED, OWNED)], own_sem.at[r]
        )

    def scatter(r, k):
        return pltpu.make_async_remote_copy(
            src_ref=part.at[r, peer(k)], dst_ref=arrived.at[r, k],
            send_sem=tile_send.at[r, k], recv_sem=tile_recv.at[r, k],
            device_id={"tile": peer(k)}, device_id_type=MESH,
        )

    loads = [
        pltpu.make_async_copy(bases, bases_v, load_sem.at[0]),
        pltpu.make_async_copy(cols, cols_v, load_sem.at[1]),
        pltpu.make_async_copy(diag, diag_v, load_sem.at[2]),
        pltpu.make_async_copy(right_side, right_v, load_sem.at[3]),
    ]

    for i in (0, 1):
        for way in (0, 1):
            ring(0, i, way).start()
    pair_own(0, core).start()
    keep_own(0).start()
    for load in loads:
        load.start()
    for r in range(CHUNKS):
        blocks[r][NBLK] = jnp.zeros((BLOCK, WIDTH), jnp.bfloat16)

    def slot(c, q):
        s = c * SEG + q
        return jnp.where(q < counts[front, c], ids[front, s], NBLK)

    def sums(r, dy):
        to_y = (y + dy) % NY
        rows = pl.ds(pl.multiple_of(to_y * GROUP, GROUP), GROUP)
        for c in range(FRONTS):
            total = jnp.zeros((GROUP, WIDTH), jnp.float32)
            for q in range(SEG):
                total += jnp.dot(
                    bases_v[c, q, rows, :], blocks[r][slot(c, q)], preferred_element_type=jnp.float32
                )
            part[r, pl.ds(to_y * NX, NX), c] = total.astype(jnp.bfloat16).reshape(NX, RANK, WIDTH)
        for dx in range(NX):
            k = dy * NX + dx
            if k:
                scatter(r, k).start()

    def chunk_ready(r):
        for i in range(NP):
            for way in (0, 1):
                pair(r, i, way, 1 - core).wait_recv()
        pair_own(r, 1 - core).wait_recv()
        keep_own(r).wait()
        if r == 0:
            loads[0].wait()

    def out_copy(r):
        return pltpu.make_async_copy(out_v.at[r], out.at[:, :, chunk_cols(r)], out_sem.at[r])

    def finish(r):
        if r == 0:
            for load in loads[1:]:
                load.wait()
        for k in range(1, NT):
            scatter(r, k).wait_recv()
        arrived[r, 0] = part[r, tile]
        for c in range(FRONTS):
            total = jnp.sum(arrived[r, :, c].astype(jnp.float32), axis=0)
            row = lax.broadcasted_iota(jnp.int32, (RANK, WIDTH), 0)
            rank_space = jnp.where(row < ranks[c], total, 0.0).astype(jnp.bfloat16)
            projected = lax.dot_general(
                cols_v[c], rank_space, (((0,), (0,)), ((), ())), preferred_element_type=jnp.float32
            )
            reduced = (right_v[c, :, chunk_cols(r)].astype(jnp.float32) - projected).astype(jnp.bfloat16)
            out_v[r, c] = jnp.dot(
                diag_v[c], reduced, preferred_element_type=jnp.float32
            ).astype(jnp.bfloat16)
        out_copy(r).start()

    def sent(r):
        for i in range(NP):
            for way in (0, 1):
                ring(r, i, way).wait_send()
                pair(r, i, way, core).wait_send()
        pair_own(r, core).wait_send()

    order = (2, 1, 3, 0)
    for r in range(CHUNKS):
        for i in range(NP):
            for way in (0, 1):
                wait_ring(r, i, way)
                if i + 2 < NP:
                    ring(r, i + 2, way).start()
                elif r + 1 < CHUNKS:
                    ring(r + 1, i + 2 - NP, way).start()
                pair(r, i, way, core).start()
            if i == 0 and r + 1 < CHUNKS:
                pair_own(r + 1, core).start()
                keep_own(r + 1).start()
            if r >= 1:
                if i == 0:
                    chunk_ready(r - 1)
                if i < NY:
                    sums(r - 1, order[i])
            if r >= 2 and i == 4:
                finish(r - 2)
            if r >= 1 and i == 5:
                sent(r - 1)
    last = CHUNKS - 1
    chunk_ready(last)
    for dy in order:
        sums(last, dy)
    finish(last - 1)
    sent(last)
    for r in range(CHUNKS - 1):
        for k in range(1, NT):
            scatter(r, k).wait_send()
    finish(last)
    for k in range(1, NT):
        scatter(last, k).wait_send()
    for r in range(CHUNKS):
        out_copy(r).wait()


def local(
    parent_solution, segment_ids, segment_counts, row_bases, column_bases, diag_inverse, child_right, tile_ranks
):
    bases = row_bases.reshape(FRONTS, SEG, NT * RANK, BLOCK)
    whole = pl.BlockSpec(memory_space=pl.ANY)
    scalars = pl.BlockSpec(memory_space=pltpu.SMEM)
    dma = pltpu.SemaphoreType.DMA
    result = pl.pallas_call(
        kernel,
        out_shape=jax.ShapeDtypeStruct((FRONTS, BLOCK, RHS), jnp.bfloat16),
        in_specs=[scalars] * 3 + [whole] * 5,
        out_specs=whole,
        scratch_shapes=[pltpu.VMEM((NBLK + 1, BLOCK, WIDTH), jnp.bfloat16)] * CHUNKS
        + [
            pltpu.VMEM((FRONTS, SEG, NT * RANK, BLOCK), jnp.bfloat16),
            pltpu.VMEM((FRONTS, RANK, BLOCK), jnp.bfloat16),
            pltpu.VMEM((FRONTS, BLOCK, BLOCK), jnp.bfloat16),
            pltpu.VMEM((FRONTS, BLOCK, RHS), jnp.bfloat16),
            pltpu.VMEM((CHUNKS, FRONTS, BLOCK, WIDTH), jnp.bfloat16),
            pltpu.VMEM((CHUNKS, NT, FRONTS, RANK, WIDTH), jnp.bfloat16),
            pltpu.VMEM((CHUNKS, NT, FRONTS, RANK, WIDTH), jnp.bfloat16),
            dma((CHUNKS, NP, 2)),
            dma((CHUNKS, NP, 2)),
            dma((CHUNKS, NP + 1, 2)),
            dma((CHUNKS, NP + 1, 2)),
            dma((CHUNKS, NT)),
            dma((CHUNKS, NT)),
            dma((4,)),
            dma((CHUNKS,)),
            dma((CHUNKS,)),
        ],
        compiler_params=pltpu.CompilerParams(
            collective_id=0, has_side_effects=True, vmem_limit_bytes=56 * 1024 * 1024
        ),
        cost_estimate=pl.CostEstimate(
            flops=2 * FRONTS * SEG * NT * RANK * BLOCK * RHS, bytes_accessed=12 << 20, transcendentals=0
        ),
    )(
        segment_ids[0], segment_counts[0], tile_ranks.reshape(FRONTS),
        parent_solution[0], bases, column_bases[0, :, 0], diag_inverse[0, :, 0], child_right[0, :, 0],
    )
    return result[None, :, None]


def solution(mesh):
    placed = (
        P("tile", "front", None, None),
        P("tile", None, None),
        P("tile", None, None),
        P("tile", "front", None, None, None, None, None),
        P("front", None, "tile", None, None),
        P("front", None, "tile", None, None),
        P("front", None, "tile", None, None),
        P("front", None, "tile"),
    )
    return jax.shard_map(
        local,
        mesh=mesh,
        in_specs=placed,
        out_specs=P("front", None, "tile", None, None),
        check_vma=False,
    )
```

time: 394 us -> 110 us (0.28)
  waiting for transfers between devices: 278 us -> 0 us
  Pallas kernels: 0 us -> 107 us
  local copies, waits for them, and re-layouts: 62.5 us -> 3.22 us
  matrix products: 26.6 us -> 0 us
  between operations: 13.5 us -> 0.01 us
  starting transfers between devices: 10.2 us -> 0 us
    all_to_all x1 -> x0, waiting for transfers between devices: 166 us -> none  [local(): lax.all_to_all(outgoing, 'front', split_axis=0, concat_axis=0, tiled=True)]
    unnamed x2 -> x0, waiting for transfers between devices: 112 us -> none
    pallas_call x0 -> x1, Pallas kernels: none -> 107 us  [local(): pl.pallas_call(kernel, out_shape=jax.ShapeDtypeStruct((FRONTS, BLOCK, RHS...]
    dot_general x5 -> x0, matrix products: 26.6 us -> none  [the longest x1 10.9 us: local(): jnp.einsum('csjkb,csbmn->cjkmn', bases_here, gathered, preferred_element_...]
    reshape x4 -> x0, local copies, waits for them, and re-layouts: 20.2 us -> none  [the longest x1 14.6 us: local(): arrived = received.reshape(nfront * CAP, nblock, ncols // 128, 128)]
    squeeze x1, local copies, waits for them, and re-layouts: 16.9 us -> 1.35 us  [local(): segment_counts[0]]
    all_to_all x1 -> x0, local copies, waits for them, and re-layouts: 12.3 us -> none  [local(): lax.all_to_all(outgoing, 'front', split_axis=0, concat_axis=0, tiled=True)]
    convert_element_type x1 -> x0, local copies, waits for them, and re-layouts: 11.3 us -> none  [local(): outgoing = jnp.einsum('fpl,lbr->fpbr', selector, held_blocks, preferred_e...]
  transfers between devices with their start and end apart: 2 -> 0, of which waited for: 2 -> 0; matrix products, arithmetic and copies ran while one was open for 5% -> 0% of each run, Pallas kernels for 0% -> 0%
where the time goes in v1:
time: 110 us
  Pallas kernels  107 us (97%)
  local copies, waits for them, and re-layouts  3.22 us (3%)
    pallas_call x1, Pallas kernels, local(): pl.pallas_call(kernel, out_shape=jax.ShapeDtypeStruct((FRONTS, BLOCK, RHS...  107 us

profile of v1, /device:TPU:1, one launch (start us, length us, event | category | flops | bytes accessed | tf_op | source)
XLA Modules:
  0.0 109.9 jit_solution(3436655460556502673)
XLA Ops:
  0.0 1.4 %copy.9.counts = s32[16,2]{1,0:T(8,128)} copy(s32[16,2]{0,1:T(2,128)} %bitcast.12) | data formatting | bytes 256 | tf_op jit(solution)/shard_map/squeeze | solution.py:268
  1.4 106.6 %shard_map.82 = bf16[2,256,512]{2,1,0:T(8,128)(2,1)} custom-call(s32[16,16]{1,0:T(8,128)} %bitcast.18, s32[16,2]{1,0:T(8,128)} %copy.9.counts, s32[2]{0:T(128)} %bitcast.19, bf16[4,256,512]{2,1,0:T(8,128)(2,1)} %bitcast.14, bf16[2,8,1024,256]{3,2,1,0:T(8,128)(2,1)} %bitcast.13, bf16[2,64,256]{2,1,0:T(8,128)(2,1)} %bitcast.17, bf16[2,256,256]{2,1,0:T(8,128)(2,1)} %bitcast.16, ...), custom_call_target="tpu_custom_call" | custom-call | flops 4294967296 | bytes 12582912 | tf_op jit(solution)/shard_map/pallas_call | solution.py:237
  108.0 1.9 %copy.12 = bf16[1,2,1,256,512]{4,3,2,1,0:T(8,128)(2,1)} copy(bf16[1,2,1,256,512]{4,3,2,1,0:T(8,128)(2,1)} %bitcast.11) | data formatting | bytes 1048576

commit v2 on v1

--- a/solution.py
+++ b/solution.py
@@ -51,8 +51,8 @@
         pl.semaphore_signal(barrier, inc=1, device_id={"tile": peer(k)}, device_id_type=MESH)
     pl.semaphore_wait(barrier, 3 + NT - 1)
 
-    def place(chip, who, half):
-        return pl.ds((chip * 2 + who) * OWNED + half * 2, 2)
+    def place(chip, half):
+        return pl.ds((chip * 2 + core) * OWNED + half * 2, 2)
 
     def chunk_cols(r):
         return pl.ds(r * WIDTH, WIDTH)
@@ -61,44 +61,44 @@
         hop, half = PIECES[i]
         half = half if way == 0 else 1 - half
         chip = (z + NZ - (hop - 1)) % NZ if way == 0 else (z + hop - 1) % NZ
-        dst = blocks[r].at[place(chip, core, half)]
+        dst = blocks[r].at[place(chip, half)]
         if hop == 1:
             src = parent.at[pl.ds(half * 2, 2), :, chunk_cols(r)]
         else:
             src = dst
         return pltpu.make_async_remote_copy(
             src_ref=src, dst_ref=dst,
-            send_sem=ring_send.at[r, i, way], recv_sem=ring_recv.at[r, i, way],
+            send_sem=ring_send.at[r], recv_sem=ring_recv.at[r, i, way],
             device_id={"front": ahead if way == 0 else behind}, device_id_type=MESH,
         )
 
-    def ring_in(r, i, way, who):
+    def ring_in(r, i, way):
         hop, half = PIECES[i]
         half = half if way == 0 else 1 - half
         chip = (z + NZ - hop) % NZ if way == 0 else (z + hop) % NZ
-        return blocks[r].at[place(chip, who, half)]
+        return blocks[r].at[place(chip, half)]
 
     def wait_ring(r, i, way):
-        here = ring_in(r, i, way, core)
+        here = ring_in(r, i, way)
         pltpu.make_async_remote_copy(
             src_ref=here, dst_ref=here,
-            send_sem=ring_send.at[r, i, way], recv_sem=ring_recv.at[r, i, way],
+            send_sem=ring_send.at[r], recv_sem=ring_recv.at[r, i, way],
             device_id={"front": ahead}, device_id_type=MESH,
         ).wait_recv()
 
-    def pair(r, i, way, who):
-        here = ring_in(r, i, way, who)
+    def pair(r, i, way):
+        here = ring_in(r, i, way)
         return pltpu.make_async_remote_copy(
             src_ref=here, dst_ref=here,
-            send_sem=pair_send.at[r, i, way], recv_sem=pair_recv.at[r, i, way],
+            send_sem=pair_send.at[r], recv_sem=pair_recv.at[r],
             device_id={"front": sibling}, device_id_type=MESH,
         )
 
-    def pair_own(r, who):
+    def pair_own(r):
         return pltpu.make_async_remote_copy(
             src_ref=parent.at[:, :, chunk_cols(r)],
-            dst_ref=blocks[r].at[pl.ds((z * 2 + who) * OWNED, OWNED)],
-            send_sem=pair_send.at[r, NP, 0], recv_sem=pair_recv.at[r, NP, 0],
+            dst_ref=blocks[r].at[pl.ds(front * OWNED, OWNED)],
+            send_sem=pair_send.at[r], recv_sem=pair_recv.at[r],
             device_id={"front": sibling}, device_id_type=MESH,
         )
 
@@ -107,10 +107,25 @@
             parent.at[:, :, chunk_cols(r)], blocks[r].at[pl.ds(front * OWNED, OWNED)], own_sem.at[r]
         )
 
+    def all_of(ref, send, recv):
+        return pltpu.make_async_remote_copy(
+            src_ref=ref, dst_ref=ref, send_sem=send, recv_sem=recv,
+            device_id={"front": sibling}, device_id_type=MESH,
+        )
+
+    def all_ring(r):
+        return all_of(blocks[r].at[pl.ds(0, 4 * NP)], ring_send.at[r], ring_recv.at[r, 0, 0])
+
+    def all_pair(r):
+        return all_of(blocks[r].at[pl.ds(0, 4 * NP + OWNED)], pair_send.at[r], pair_recv.at[r])
+
+    def all_scatter(r):
+        return all_of(arrived.at[r, pl.ds(1, NT - 1)], tile_send.at[r], tile_recv.at[r])
+
     def scatter(r, k):
         return pltpu.make_async_remote_copy(
             src_ref=part.at[r, peer(k)], dst_ref=arrived.at[r, k],
-            send_sem=tile_send.at[r, k], recv_sem=tile_recv.at[r, k],
+            send_sem=tile_send.at[r], recv_sem=tile_recv.at[r],
             device_id={"tile": peer(k)}, device_id_type=MESH,
         )
 
@@ -124,7 +139,7 @@
     for i in (0, 1):
         for way in (0, 1):
             ring(0, i, way).start()
-    pair_own(0, core).start()
+    pair_own(0).start()
     keep_own(0).start()
     for load in loads:
         load.start()
@@ -133,7 +148,7 @@
 
     def slot(c, q):
         s = c * SEG + q
-        return jnp.where(q < counts[front, c], ids[front, s], NBLK)
+        return jnp.where(q < counts[c, front], ids[front, s], NBLK)
 
     def sums(r, dy):
         to_y = (y + dy) % NY
@@ -151,10 +166,7 @@
                 scatter(r, k).start()
 
     def chunk_ready(r):
-        for i in range(NP):
-            for way in (0, 1):
-                pair(r, i, way, 1 - core).wait_recv()
-        pair_own(r, 1 - core).wait_recv()
+        all_pair(r).wait_recv()
         keep_own(r).wait()
         if r == 0:
             loads[0].wait()
@@ -166,8 +178,7 @@
         if r == 0:
             for load in loads[1:]:
                 load.wait()
-        for k in range(1, NT):
-            scatter(r, k).wait_recv()
+        all_scatter(r).wait_recv()
         arrived[r, 0] = part[r, tile]
         for c in range(FRONTS):
             total = jnp.sum(arrived[r, :, c].astype(jnp.float32), axis=0)
@@ -183,11 +194,8 @@
         out_copy(r).start()
 
     def sent(r):
-        for i in range(NP):
-            for way in (0, 1):
-                ring(r, i, way).wait_send()
-                pair(r, i, way, core).wait_send()
-        pair_own(r, core).wait_send()
+        all_ring(r).wait_send()
+        all_pair(r).wait_send()
 
     order = (2, 1, 3, 0)
     for r in range(CHUNKS):
@@ -198,9 +206,9 @@
                     ring(r, i + 2, way).start()
                 elif r + 1 < CHUNKS:
                     ring(r + 1, i + 2 - NP, way).start()
-                pair(r, i, way, core).start()
+                pair(r, i, way).start()
             if i == 0 and r + 1 < CHUNKS:
-                pair_own(r + 1, core).start()
+                pair_own(r + 1).start()
                 keep_own(r + 1).start()
             if r >= 1:
                 if i == 0:
@@ -218,11 +226,9 @@
     finish(last - 1)
     sent(last)
     for r in range(CHUNKS - 1):
-        for k in range(1, NT):
-            scatter(r, k).wait_send()
+        all_scatter(r).wait_send()
     finish(last)
-    for k in range(1, NT):
-        scatter(last, k).wait_send()
+    all_scatter(last).wait_send()
     for r in range(CHUNKS):
         out_copy(r).wait()
 
@@ -248,12 +254,12 @@
             pltpu.VMEM((CHUNKS, FRONTS, BLOCK, WIDTH), jnp.bfloat16),
             pltpu.VMEM((CHUNKS, NT, FRONTS, RANK, WIDTH), jnp.bfloat16),
             pltpu.VMEM((CHUNKS, NT, FRONTS, RANK, WIDTH), jnp.bfloat16),
+            dma((CHUNKS,)),
             dma((CHUNKS, NP, 2)),
-            dma((CHUNKS, NP, 2)),
-            dma((CHUNKS, NP + 1, 2)),
-            dma((CHUNKS, NP + 1, 2)),
-            dma((CHUNKS, NT)),
-            dma((CHUNKS, NT)),
+            dma((CHUNKS,)),
+            dma((CHUNKS,)),
+            dma((CHUNKS,)),
+            dma((CHUNKS,)),
             dma((4,)),
             dma((CHUNKS,)),
             dma((CHUNKS,)),
@@ -265,7 +271,7 @@
             flops=2 * FRONTS * SEG * NT * RANK * BLOCK * RHS, bytes_accessed=12 << 20, transcendentals=0
         ),
     )(
-        segment_ids[0], segment_counts[0], tile_ranks.reshape(FRONTS),
+        segment_ids[0], segment_counts[0].T, tile_ranks.reshape(FRONTS),
         parent_solution[0], bases, column_bases[0, :, 0], diag_inverse[0, :, 0], child_right[0, :, 0],
     )
     return result[None, :, None]

time: 110 us -> 106 us (0.964)
  Pallas kernels: 107 us -> 104 us
  local copies, waits for them, and re-layouts: 3.22 us -> 1.87 us
    pallas_call x1, Pallas kernels: 107 us -> 104 us  [local(): pl.pallas_call(kernel, out_shape=jax.ShapeDtypeStruct((FRONTS, BLOCK, RHS...]
    squeeze x1 -> x0, local copies, waits for them, and re-layouts: 1.35 us -> none  [local(): segment_counts[0]]
where the time goes in v2:
time: 106 us
  Pallas kernels  104 us (98%)
  local copies, waits for them, and re-layouts  1.87 us (2%)
    pallas_call x1, Pallas kernels, local(): pl.pallas_call(kernel, out_shape=jax.ShapeDtypeStruct((FRONTS, BLOCK, RHS...  104 us

profile of v2, /device:TPU:1, one launch (start us, length us, event | category | flops | bytes accessed | tf_op | source)
XLA Modules:
  0.0 105.7 jit_solution(10025776548625141440)
XLA Ops:
  0.0 103.9 %shard_map.82 = bf16[2,256,512]{2,1,0:T(8,128)(2,1)} custom-call(s32[16,16]{1,0:T(8,128)} %bitcast.19, s32[2,16]{1,0:T(2,128)} %bitcast.20, s32[2]{0:T(128)} %bitcast.21, bf16[4,256,512]{2,1,0:T(8,128)(2,1)} %bitcast.15, bf16[2,8,1024,256]{3,2,1,0:T(8,128)(2,1)} %bitcast.14, bf16[2,64,256]{2,1,0:T(8,128)(2,1)} %bitcast.18, bf16[2,256,256]{2,1,0:T(8,128)(2,1)} %bitcast.17, ...), custom_call_target="tpu_custom_call" | custom-call | flops 4294967296 | bytes 12582912 | tf_op jit(solution)/shard_map/pallas_call | solution.py:243
  103.9 1.9 %copy.11 = bf16[1,2,1,256,512]{4,3,2,1,0:T(8,128)(2,1)} copy(bf16[1,2,1,256,512]{4,3,2,1,0:T(8,128)(2,1)} %bitcast.13) | data formatting | bytes 1048576

commit v3 on v2

--- a/solution.py
+++ b/solution.py
@@ -29,8 +29,8 @@
 
 def kernel(
     ids, counts, ranks, parent, bases, cols, diag, right_side, out,
-    b0, b1, b2, b3, bases_v, cols_v, diag_v, right_v, out_v, part, arrived,
-    ring_send, ring_recv, pair_send, pair_recv, tile_send, tile_recv, load_sem, own_sem, out_sem,
+    b0, b1, b2, b3, bases_v, cols_v, diag_v, right_v, part, arrived,
+    ring_send, ring_recv, pair_send, pair_recv, tile_send, tile_recv, load_sem, own_sem, row_sem,
 ):
     blocks = (b0, b1, b2, b3)
     front = lax.axis_index("front")
@@ -47,9 +47,18 @@
     barrier = pltpu.get_barrier_semaphore()
     for other in (ahead, behind, sibling):
         pl.semaphore_signal(barrier, inc=1, device_id={"front": other}, device_id_type=MESH)
-    for k in range(1, NT):
-        pl.semaphore_signal(barrier, inc=1, device_id={"tile": peer(k)}, device_id_type=MESH)
-    pl.semaphore_wait(barrier, 3 + NT - 1)
+    along_x = (peer(1), peer(NX - 1))
+    along_y = (peer(NX), peer((NY - 1) * NX))
+    for other in along_x + along_y:
+        pl.semaphore_signal(barrier, inc=1, device_id={"tile": other}, device_id_type=MESH)
+    pl.semaphore_wait(barrier, 3 + 4)
+
+    def tell(step):
+        for other in along_x if step == 0 else along_y:
+            pl.semaphore_signal(row_sem.at[step], inc=1, device_id={"tile": other}, device_id_type=MESH)
+
+    def told(step):
+        pl.semaphore_wait(row_sem.at[step], 2)
 
     def place(chip, half):
         return pl.ds((chip * 2 + core) * OWNED + half * 2, 2)
@@ -143,6 +152,7 @@
     keep_own(0).start()
     for load in loads:
         load.start()
+    tell(0)
     for r in range(CHUNKS):
         blocks[r][NBLK] = jnp.zeros((BLOCK, WIDTH), jnp.bfloat16)
 
@@ -171,9 +181,6 @@
         if r == 0:
             loads[0].wait()
 
-    def out_copy(r):
-        return pltpu.make_async_copy(out_v.at[r], out.at[:, :, chunk_cols(r)], out_sem.at[r])
-
     def finish(r):
         if r == 0:
             for load in loads[1:]:
@@ -188,10 +195,9 @@
                 cols_v[c], rank_space, (((0,), (0,)), ((), ())), preferred_element_type=jnp.float32
             )
             reduced = (right_v[c, :, chunk_cols(r)].astype(jnp.float32) - projected).astype(jnp.bfloat16)
-            out_v[r, c] = jnp.dot(
+            out[c, :, chunk_cols(r)] = jnp.dot(
                 diag_v[c], reduced, preferred_element_type=jnp.float32
             ).astype(jnp.bfloat16)
-        out_copy(r).start()
 
     def sent(r):
         all_ring(r).wait_send()
@@ -207,6 +213,10 @@
                 elif r + 1 < CHUNKS:
                     ring(r + 1, i + 2 - NP, way).start()
                 pair(r, i, way).start()
+            if r == 0 and i < 3:
+                told(i)
+                if i < 2:
+                    tell(i + 1)
             if i == 0 and r + 1 < CHUNKS:
                 pair_own(r + 1).start()
                 keep_own(r + 1).start()
@@ -229,8 +239,6 @@
         all_scatter(r).wait_send()
     finish(last)
     all_scatter(last).wait_send()
-    for r in range(CHUNKS):
-        out_copy(r).wait()
 
 
 def local(
@@ -242,16 +250,15 @@
     dma = pltpu.SemaphoreType.DMA
     result = pl.pallas_call(
         kernel,
-        out_shape=jax.ShapeDtypeStruct((FRONTS, BLOCK, RHS), jnp.bfloat16),
+        out_shape=pltpu.VMEM((FRONTS, BLOCK, RHS), jnp.bfloat16),
         in_specs=[scalars] * 3 + [whole] * 5,
-        out_specs=whole,
+        out_specs=pl.BlockSpec(memory_space=pltpu.VMEM),
         scratch_shapes=[pltpu.VMEM((NBLK + 1, BLOCK, WIDTH), jnp.bfloat16)] * CHUNKS
         + [
             pltpu.VMEM((FRONTS, SEG, NT * RANK, BLOCK), jnp.bfloat16),
             pltpu.VMEM((FRONTS, RANK, BLOCK), jnp.bfloat16),
             pltpu.VMEM((FRONTS, BLOCK, BLOCK), jnp.bfloat16),
             pltpu.VMEM((FRONTS, BLOCK, RHS), jnp.bfloat16),
-            pltpu.VMEM((CHUNKS, FRONTS, BLOCK, WIDTH), jnp.bfloat16),
             pltpu.VMEM((CHUNKS, NT, FRONTS, RANK, WIDTH), jnp.bfloat16),
             pltpu.VMEM((CHUNKS, NT, FRONTS, RANK, WIDTH), jnp.bfloat16),
             dma((CHUNKS,)),
@@ -262,7 +269,7 @@
             dma((CHUNKS,)),
             dma((4,)),
             dma((CHUNKS,)),
-            dma((CHUNKS,)),
+            pltpu.SemaphoreType.REGULAR((3,)),
         ],
         compiler_params=pltpu.CompilerParams(
             collective_id=0, has_side_effects=True, vmem_limit_bytes=56 * 1024 * 1024

time: 106 us -> 103 us (0.972)
  Pallas kernels: 104 us -> 102 us
  local copies, waits for them, and re-layouts: 1.87 us -> 0.8 us
    pallas_call x1, Pallas kernels: 104 us -> 102 us  [local(): pl.pallas_call(kernel, out_shape=pltpu.VMEM((FRONTS, BLOCK, RHS), jnp.bfl...]
    unnamed x1, local copies, waits for them, and re-layouts: 1.87 us -> 0.8 us
where the time goes in v3:
time: 103 us
  Pallas kernels  102 us (99%)
    pallas_call x1, Pallas kernels, local(): pl.pallas_call(kernel, out_shape=pltpu.VMEM((FRONTS, BLOCK, RHS), jnp.bfl...  102 us

profile of v3, /device:TPU:1, one launch (start us, length us, event | category | flops | bytes accessed | tf_op | source)
XLA Modules:
  0.0 102.9 jit_solution(2720396035913714053)
XLA Ops:
  0.0 102.0 %shard_map.82 = bf16[2,256,512]{2,1,0:T(8,128)(2,1)S(1)} custom-call(s32[16,16]{1,0:T(8,128)} %bitcast.19, s32[2,16]{1,0:T(2,128)} %bitcast.20, s32[2]{0:T(128)} %bitcast.21, bf16[4,256,512]{2,1,0:T(8,128)(2,1)} %bitcast.15, bf16[2,8,1024,256]{3,2,1,0:T(8,128)(2,1)} %bitcast.14, bf16[2,64,256]{2,1,0:T(8,128)(2,1)} %bitcast.18, ...), custom_call_target="tpu_custom_call" | custom-call | flops 4294967296 | bytes 12582912 | tf_op jit(solution)/shard_map/pallas_call | solution.py:251
  102.1 0.8 copy.11

commit v4 on v3

--- a/solution.py
+++ b/solution.py
@@ -49,9 +49,14 @@
         pl.semaphore_signal(barrier, inc=1, device_id={"front": other}, device_id_type=MESH)
     along_x = (peer(1), peer(NX - 1))
     along_y = (peer(NX), peer((NY - 1) * NX))
-    for other in along_x + along_y:
-        pl.semaphore_signal(barrier, inc=1, device_id={"tile": other}, device_id_type=MESH)
-    pl.semaphore_wait(barrier, 3 + 4)
+    ground = z == 0
+
+    @pl.when(ground)
+    def _():
+        for other in along_x + along_y:
+            pl.semaphore_signal(barrier, inc=1, device_id={"tile": other}, device_id_type=MESH)
+
+    pl.semaphore_wait(barrier, jnp.where(ground, 3 + 4, 3))
 
     def tell(step):
         for other in along_x if step == 0 else along_y:
@@ -59,6 +64,19 @@
 
     def told(step):
         pl.semaphore_wait(row_sem.at[step], 2)
+        if step < 2:
+            tell(step + 1)
+
+    def column_entered():
+        for k in range(1, NT):
+            pl.semaphore_signal(row_sem.at[3], inc=1, device_id={"tile": peer(k)}, device_id_type=MESH)
+
+    def all_entered():
+        pl.semaphore_wait(row_sem.at[3], NT - 1)
+        for chip in range(1, NZ):
+            pl.semaphore_signal(
+                row_sem.at[4], inc=1, device_id={"front": chip * 2 + core}, device_id_type=MESH
+            )
 
     def place(chip, half):
         return pl.ds((chip * 2 + core) * OWNED + half * 2, 2)
@@ -152,7 +170,7 @@
     keep_own(0).start()
     for load in loads:
         load.start()
-    tell(0)
+    pl.when(ground)(lambda: tell(0))
     for r in range(CHUNKS):
         blocks[r][NBLK] = jnp.zeros((BLOCK, WIDTH), jnp.bfloat16)
 
@@ -214,17 +232,22 @@
                     ring(r + 1, i + 2 - NP, way).start()
                 pair(r, i, way).start()
             if r == 0 and i < 3:
-                told(i)
-                if i < 2:
-                    tell(i + 1)
+                pl.when(ground)(functools.partial(told, i))
+            if (r, i) == (0, 6):
+                pl.when(ground)(column_entered)
+            if (r, i) == (1, 1):
+                pl.when(ground)(all_entered)
+            if (r, i) == (1, 3):
+                pl.when(z > 0)(lambda: pl.semaphore_wait(row_sem.at[4], 1))
             if i == 0 and r + 1 < CHUNKS:
                 pair_own(r + 1).start()
                 keep_own(r + 1).start()
             if r >= 1:
                 if i == 0:
                     chunk_ready(r - 1)
-                if i < NY:
-                    sums(r - 1, order[i])
+                after = 3 if r == 1 else 0
+                if after <= i < after + NY:
+                    sums(r - 1, order[i - after])
             if r >= 2 and i == 4:
                 finish(r - 2)
             if r >= 1 and i == 5:
@@ -269,7 +292,7 @@
             dma((CHUNKS,)),
             dma((4,)),
             dma((CHUNKS,)),
-            pltpu.SemaphoreType.REGULAR((3,)),
+            pltpu.SemaphoreType.REGULAR((5,)),
         ],
         compiler_params=pltpu.CompilerParams(
             collective_id=0, has_side_effects=True, vmem_limit_bytes=56 * 1024 * 1024

time: 103 us -> 101 us (0.981)
  Pallas kernels: 102 us -> 100 us
    pallas_call x1, Pallas kernels: 102 us -> 100 us  [local(): pl.pallas_call(kernel, out_shape=pltpu.VMEM((FRONTS, BLOCK, RHS), jnp.bfl...]
where the time goes in v4:
time: 101 us
  Pallas kernels  100 us (99%)
    pallas_call x1, Pallas kernels, local(): pl.pallas_call(kernel, out_shape=pltpu.VMEM((FRONTS, BLOCK, RHS), jnp.bfl...  100 us

profile of v4, /device:TPU:1, one launch (start us, length us, event | category | flops | bytes accessed | tf_op | source)
XLA Modules:
  0.0 101.3 jit_solution(8512643380271319263)
XLA Ops:
  0.0 100.5 %shard_map.82 = bf16[2,256,512]{2,1,0:T(8,128)(2,1)S(1)} custom-call(s32[16,16]{1,0:T(8,128)} %bitcast.19, s32[2,16]{1,0:T(2,128)} %bitcast.20, s32[2]{0:T(128)} %bitcast.21, bf16[4,256,512]{2,1,0:T(8,128)(2,1)} %bitcast.15, bf16[2,8,1024,256]{3,2,1,0:T(8,128)(2,1)} %bitcast.14, bf16[2,64,256]{2,1,0:T(8,128)(2,1)} %bitcast.18, ...), custom_call_target="tpu_custom_call" | custom-call | flops 4294967296 | bytes 12582912 | tf_op jit(solution)/shard_map/pallas_call | solution.py:274
  100.5 0.8 copy.11

commit v5 on v4

--- a/solution.py
+++ b/solution.py
@@ -23,8 +23,9 @@
 CHUNKS = RHS // WIDTH
 NBLK = NZ * 2 * OWNED
 GROUP = NX * RANK
-PIECES = ((1, 0), (1, 1), (2, 0), (2, 1), (3, 0), (3, 1), (4, 0))
+PIECES = ((1, 0, 2), (1, 2, 2), (2, 0, 2), (2, 2, 2), (3, 0, 2), (3, 2, 2), (4, 0, 2))
 NP = len(PIECES)
+LAST_PIECES = PIECES[:-1] + ((4, 0, 1), (4, 1, 1))
 
 
 def kernel(
@@ -78,38 +79,43 @@
                 row_sem.at[4], inc=1, device_id={"front": chip * 2 + core}, device_id_type=MESH
             )
 
-    def place(chip, half):
-        return pl.ds((chip * 2 + core) * OWNED + half * 2, 2)
+    def place(chip, first, size):
+        return pl.ds((chip * 2 + core) * OWNED + first, size)
+
+    def pieces(r):
+        return PIECES if r < CHUNKS - 1 else LAST_PIECES
+
+    def piece(r, i, way):
+        hop, first, size = pieces(r)[i]
+        return hop, first if way == 0 else OWNED - first - size, size
 
     def chunk_cols(r):
         return pl.ds(r * WIDTH, WIDTH)
 
     def ring(r, i, way):
-        hop, half = PIECES[i]
-        half = half if way == 0 else 1 - half
+        hop, first, size = piece(r, i, way)
         chip = (z + NZ - (hop - 1)) % NZ if way == 0 else (z + hop - 1) % NZ
-        dst = blocks[r].at[place(chip, half)]
+        dst = blocks[r].at[place(chip, first, size)]
         if hop == 1:
-            src = parent.at[pl.ds(half * 2, 2), :, chunk_cols(r)]
+            src = parent.at[pl.ds(first, size), :, chunk_cols(r)]
         else:
             src = dst
         return pltpu.make_async_remote_copy(
             src_ref=src, dst_ref=dst,
-            send_sem=ring_send.at[r], recv_sem=ring_recv.at[r, i, way],
+            send_sem=ring_send.at[r], recv_sem=ring_recv.at[r % 2, i, way],
             device_id={"front": ahead if way == 0 else behind}, device_id_type=MESH,
         )
 
     def ring_in(r, i, way):
-        hop, half = PIECES[i]
-        half = half if way == 0 else 1 - half
+        hop, first, size = piece(r, i, way)
         chip = (z + NZ - hop) % NZ if way == 0 else (z + hop) % NZ
-        return blocks[r].at[place(chip, half)]
+        return blocks[r].at[place(chip, first, size)]
 
     def wait_ring(r, i, way):
         here = ring_in(r, i, way)
         pltpu.make_async_remote_copy(
             src_ref=here, dst_ref=here,
-            send_sem=ring_send.at[r], recv_sem=ring_recv.at[r, i, way],
+            send_sem=ring_send.at[r], recv_sem=ring_recv.at[r % 2, i, way],
             device_id={"front": ahead}, device_id_type=MESH,
         ).wait_recv()
 
@@ -141,7 +147,7 @@
         )
 
     def all_ring(r):
-        return all_of(blocks[r].at[pl.ds(0, 4 * NP)], ring_send.at[r], ring_recv.at[r, 0, 0])
+        return all_of(blocks[r].at[pl.ds(0, 4 * NP)], ring_send.at[r], ring_recv.at[r % 2, 0, 0])
 
     def all_pair(r):
         return all_of(blocks[r].at[pl.ds(0, 4 * NP + OWNED)], pair_send.at[r], pair_recv.at[r])
@@ -223,11 +229,13 @@
 
     order = (2, 1, 3, 0)
     for r in range(CHUNKS):
-        for i in range(NP):
+        for i in range(len(pieces(r))):
             for way in (0, 1):
                 wait_ring(r, i, way)
                 if i + 2 < NP:
                     ring(r, i + 2, way).start()
+                    if i + 3 == NP and r + 1 == CHUNKS:
+                        ring(r, NP, way).start()
                 elif r + 1 < CHUNKS:
                     ring(r + 1, i + 2 - NP, way).start()
                 pair(r, i, way).start()
@@ -285,7 +293,7 @@
             pltpu.VMEM((CHUNKS, NT, FRONTS, RANK, WIDTH), jnp.bfloat16),
             pltpu.VMEM((CHUNKS, NT, FRONTS, RANK, WIDTH), jnp.bfloat16),
             dma((CHUNKS,)),
-            dma((CHUNKS, NP, 2)),
+            dma((2, NP + 1, 2)),
             dma((CHUNKS,)),
             dma((CHUNKS,)),
             dma((CHUNKS,)),

time: 101 us -> 101 us (level)
  no operation moved by 1% of the time
where the time goes in v5:
time: 101 us
  Pallas kernels  100 us (99%)
    pallas_call x1, Pallas kernels, local(): pl.pallas_call(kernel, out_shape=pltpu.VMEM((FRONTS, BLOCK, RHS), jnp.bfl...  100 us

profile of v5, /device:TPU:1, one launch (start us, length us, event | category | flops | bytes accessed | tf_op | source)
XLA Modules:
  0.0 101.1 jit_solution(18235492410427927402)
XLA Ops:
  0.0 100.3 %shard_map.82 = bf16[2,256,512]{2,1,0:T(8,128)(2,1)S(1)} custom-call(s32[16,16]{1,0:T(8,128)} %bitcast.19, s32[2,16]{1,0:T(2,128)} %bitcast.20, s32[2]{0:T(128)} %bitcast.21, bf16[4,256,512]{2,1,0:T(8,128)(2,1)} %bitcast.15, bf16[2,8,1024,256]{3,2,1,0:T(8,128)(2,1)} %bitcast.14, bf16[2,64,256]{2,1,0:T(8,128)(2,1)} %bitcast.18, ...), custom_call_target="tpu_custom_call" | custom-call | flops 4294967296 | bytes 12582912 | tf_op jit(solution)/shard_map/pallas_call | solution.py:282
  100.3 0.8 copy.11

commit v6 on v4

--- a/solution.py
+++ b/solution.py
@@ -95,7 +95,7 @@
             src = dst
         return pltpu.make_async_remote_copy(
             src_ref=src, dst_ref=dst,
-            send_sem=ring_send.at[r], recv_sem=ring_recv.at[r, i, way],
+            send_sem=ring_send.at[r], recv_sem=ring_recv.at[r % 2, i, way],
             device_id={"front": ahead if way == 0 else behind}, device_id_type=MESH,
         )
 
@@ -109,7 +109,7 @@
         here = ring_in(r, i, way)
         pltpu.make_async_remote_copy(
             src_ref=here, dst_ref=here,
-            send_sem=ring_send.at[r], recv_sem=ring_recv.at[r, i, way],
+            send_sem=ring_send.at[r], recv_sem=ring_recv.at[r % 2, i, way],
             device_id={"front": ahead}, device_id_type=MESH,
         ).wait_recv()
 
@@ -141,7 +141,7 @@
         )
 
     def all_ring(r):
-        return all_of(blocks[r].at[pl.ds(0, 4 * NP)], ring_send.at[r], ring_recv.at[r, 0, 0])
+        return all_of(blocks[r].at[pl.ds(0, 4 * NP)], ring_send.at[r], ring_recv.at[r % 2, 0, 0])
 
     def all_pair(r):
         return all_of(blocks[r].at[pl.ds(0, 4 * NP + OWNED)], pair_send.at[r], pair_recv.at[r])
@@ -285,7 +285,7 @@
             pltpu.VMEM((CHUNKS, NT, FRONTS, RANK, WIDTH), jnp.bfloat16),
             pltpu.VMEM((CHUNKS, NT, FRONTS, RANK, WIDTH), jnp.bfloat16),
             dma((CHUNKS,)),
-            dma((CHUNKS, NP, 2)),
+            dma((2, NP, 2)),
             dma((CHUNKS,)),
             dma((CHUNKS,)),
             dma((CHUNKS,)),

time: 101 us -> 101 us (level)
  no operation moved by 1% of the time
where the time goes in v6:
time: 101 us
  Pallas kernels  100 us (99%)
    pallas_call x1, Pallas kernels, local(): pl.pallas_call(kernel, out_shape=pltpu.VMEM((FRONTS, BLOCK, RHS), jnp.bfl...  100 us

profile of v6, /device:TPU:1, one launch (start us, length us, event | category | flops | bytes accessed | tf_op | source)
XLA Modules:
  0.0 101.0 jit_solution(15035920818373982222)
XLA Ops:
  0.0 100.2 %shard_map.82 = bf16[2,256,512]{2,1,0:T(8,128)(2,1)S(1)} custom-call(s32[16,16]{1,0:T(8,128)} %bitcast.19, s32[2,16]{1,0:T(2,128)} %bitcast.20, s32[2]{0:T(128)} %bitcast.21, bf16[4,256,512]{2,1,0:T(8,128)(2,1)} %bitcast.15, bf16[2,8,1024,256]{3,2,1,0:T(8,128)(2,1)} %bitcast.14, bf16[2,64,256]{2,1,0:T(8,128)(2,1)} %bitcast.18, ...), custom_call_target="tpu_custom_call" | custom-call | flops 4294967296 | bytes 12582912 | tf_op jit(solution)/shard_map/pallas_call | solution.py:274
  100.2 0.8 copy.11
